TPU v7x, 128 devices: a whole 4x4x4 slice. The times are simulated.
128 devices in a mesh: scene: 8 (over y, core), frame: 16 (over z, x).
Axes of the slice: x: 4, y: 4, z: 4, core: 2. Of those that a mesh axis runs over, the one named last changes fastest.
Arguments:
- occupancy: bfloat16 [8, 64, 64, 2048], P('scene', 'frame'), may hold values from -6 to 6
- scene_lengths: int32 [8], P('scene'), may hold values from 8 to 64, as said below
- conv1_weight: bfloat16 [128, 1728], replicated, may hold values from -0.15625 to 0.15625
- conv2_weight: bfloat16 [256, 3456], replicated, may hold values from -0.109375 to 0.109375
- temporal_weight: bfloat16 [3, 256, 256], replicated, may hold values from -0.21875 to 0.21875
- query_weight: bfloat16 [256, 256], replicated
- key_weight: bfloat16 [256, 256], replicated
- value_weight: bfloat16 [256, 256], replicated, may hold values from -0.375 to 0.375
- out_weight: bfloat16 [256, 256], replicated, may hold values from -0.375 to 0.375
Outputs:
- encoded: bfloat16 [8, 64, 256, 512], P('scene', 'frame')
- kl_loss: float32 [], replicated
Inputs may be any that keep to these rules, and one draw needn't show every extreme that they name: `scene_lengths`: non-decreasing along the scenes; the first scene has exactly 8 frames with data and the last exactly 64.
All inputs are finite; a program needn't handle non-finite values.
Results may differ from a plain program's by a relative error of at most 0.011.
Values may be sent and summed in bfloat16 or wider, within the bound.
A program may use at most 192 MiB of HBM per device.

v0:
```python
import jax
import jax.numpy as jnp
from jax import lax
from jax.sharding import PartitionSpec as P

CIN = 64
C1 = 128
C2 = 256
HEADS = 4
HD = 64
HI = 16
ZD = 8
CELLS = 512
NORM_EPS = 1e-06


def extended(cells, sides, width):
    for axis, dim in sides:
        count = lax.axis_size(axis)
        ends = count - 1
        head = lax.slice_in_dim(cells, 0, width, axis=dim)
        tail = lax.slice_in_dim(cells, cells.shape[dim] - width, cells.shape[dim], axis=dim)
        cells = jnp.concatenate(
            [
                lax.ppermute(tail, axis, [(i, (i + 1) % count) for i in range(ends)]),
                cells,
                lax.ppermute(head, axis, [((i + 1) % count, i) for i in range(ends)]),
            ],
            axis=dim,
        )
    return cells


def spatial_conv(voxels, weight, channels_in, stride):
    channels_out = weight.shape[0]
    kernel = weight.reshape(channels_out, channels_in, 3, 3, 3)
    return lax.conv_general_dilated(
        voxels,
        kernel,
        (stride, stride, 1),
        ((1, 1), (1, 1), (1, 1)),
        dimension_numbers=("NCDHW", "OIDHW", "NCDHW"),
        preferred_element_type=jnp.float32,
    )


def mix_channels(weight, maps):
    return jnp.einsum("oc,fcn->fon", weight, maps, preferred_element_type=jnp.float32)


def temporal_block(padded, second_maps, temporal_weight):
    count_frames = second_maps.shape[0]
    temporal_sum = mix_channels(temporal_weight[0], padded[0:count_frames])
    for tap in range(1, 3):
        temporal_sum = temporal_sum + mix_channels(
            temporal_weight[tap], padded[tap : tap + count_frames]
        )
    residual_maps = (second_maps.astype(jnp.float32) + jax.nn.silu(temporal_sum)).astype(
        jnp.bfloat16
    )
    return residual_maps.astype(jnp.float32)


def project_rows(residual_f, query_weight, key_weight, value_weight):
    count_frames = residual_f.shape[0]
    count_cells = residual_f.shape[2]
    normed = (
        residual_f * lax.rsqrt(jnp.mean(residual_f * residual_f, axis=1, keepdims=True) + NORM_EPS)
    ).astype(jnp.bfloat16)
    queries = (
        mix_channels(query_weight, normed)
        .astype(jnp.bfloat16)
        .reshape(count_frames, HEADS, HD, count_cells)
    )
    key_rows = (
        mix_channels(key_weight, normed)
        .astype(jnp.bfloat16)
        .reshape(count_frames, HEADS, HD, count_cells)
    )
    value_rows = (
        mix_channels(value_weight, normed)
        .astype(jnp.bfloat16)
        .reshape(count_frames, HEADS, HD, count_cells)
    )
    return (queries, key_rows, value_rows)


def finish_rows(residual_f, attended, out_weight, valid_rows):
    count_frames = residual_f.shape[0]
    count_cells = residual_f.shape[2]
    out_full = residual_f + mix_channels(
        out_weight, attended.reshape(count_frames, C2, count_cells)
    )
    return (out_full * valid_rows[:, None, None]).astype(jnp.bfloat16)


def shards(
    occupancy,
    scene_lengths,
    conv1_weight,
    conv2_weight,
    temporal_weight,
    query_weight,
    key_weight,
    value_weight,
    out_weight,
):
    f_dev = occupancy.shape[1]
    length = scene_lengths[0]
    first_frame = lax.axis_index("frame") * f_dev
    frame_ids = first_frame + jnp.arange(f_dev, dtype=jnp.int32)
    valid_rows = (frame_ids < length).astype(jnp.float32)
    voxels = occupancy[0].reshape(f_dev, CIN, HI, HI, ZD)
    first_maps = jax.nn.silu(spatial_conv(voxels, conv1_weight, CIN, 2)).astype(jnp.bfloat16)
    second_full = jax.nn.silu(spatial_conv(first_maps, conv2_weight, C1, 1))
    second_maps = (second_full.reshape(f_dev, C2, CELLS) * valid_rows[:, None, None]).astype(
        jnp.bfloat16
    )
    padded = extended(second_maps, (("frame", 0),), 1)
    residual_f = temporal_block(padded, second_maps, temporal_weight)
    queries, key_rows, value_rows = project_rows(residual_f, query_weight, key_weight, value_weight)
    running_max = jnp.full((f_dev, HEADS, CELLS), -1e30, jnp.float32)
    panel_keys = lax.all_gather(key_rows, "frame", axis=0, tiled=True)
    panel_values = lax.all_gather(value_rows, "frame", axis=0, tiled=True)
    count_keys = panel_keys.shape[0]
    scores = jnp.einsum(
        "qhdc,khdc->qkhc", queries, panel_keys, preferred_element_type=jnp.float32
    ) * HD ** (-0.5)
    key_mask = (jnp.arange(count_keys) < length)[None, :, None, None]
    scores = jnp.where(key_mask, scores, -1e30)
    new_max = jnp.maximum(running_max, jnp.max(scores, axis=1))
    raw_weights = jnp.where(key_mask, jnp.exp(scores - new_max[:, None]), 0.0)
    new_sum = jnp.sum(raw_weights, axis=1)
    addition = jnp.einsum(
        "qkhc,khdc->qhdc",
        raw_weights.astype(jnp.bfloat16),
        panel_values,
        preferred_element_type=jnp.float32,
    )
    attended = (addition / new_sum[:, :, None, :]).astype(jnp.bfloat16)
    encoded = finish_rows(residual_f, attended, out_weight, valid_rows)
    squares = jnp.sum(jnp.square(encoded.astype(jnp.float32)))
    grand_total = lax.psum(squares, ("scene", "frame"))
    slot_count = float(lax.axis_size("scene") * lax.axis_size("frame") * f_dev * CELLS * C2)
    kl_loss = 0.5 * grand_total / slot_count
    return (encoded[None], kl_loss)


def solution(mesh):
    placed = (P("scene", "frame", None, None), P("scene"), P(), P(), P(), P(), P(), P(), P())
    return jax.shard_map(
        shards,
        mesh=mesh,
        in_specs=placed,
        out_specs=(P("scene", "frame", None, None), P()),
        check_vma=False,
    )
```

profile of v0, /device:TPU:1, one launch (start us, length us, event | category | flops | bytes accessed | tf_op | source)
XLA Modules:
  0.0 420.5 jit_solution(17460069256639030074)
XLA Ops:
  7.2 0.0 copy-start
  7.2 0.0 all-gather.5.cloned.1.call-start
  7.9 2.6 copy.62
  10.5 0.0 copy-start.3
  10.6 2.9 reshape.49
  13.4 0.0 copy-done.3
  13.4 1.1 copy.59
  14.5 1.5 reshape.48
  16.0 0.0 copy-start.1
  16.0 5.0 %fusion.28 = bf16[4,128,8,8,8]{1,0,4,3,2:T(4,128)(2,1)S(1)} fusion(bf16[4,64,16,16,8]{1,4,3,2,0:T(8,128)(2,1)S(1)} %bitcast.90, bf16[128,64,3,3,3]{0,4,3,2,1:T(4,128)(2,1)S(1)} %reshape.48), kind=kOutput, calls=%fused_computation.44 | convolution fusion | flops 764018688 | bytes 2015232 | tf_op jit(solution)/shard_map/conv_general_dilated | solution.py:37
  21.0 0.0 copy-done.1
  21.0 7.9 %multiply_convert_fusion = (bf16[4,256,8,8,8]{1,0,4,3,2:T(4,128)(2,1)S(1)}, f32[4,256,8,8,8]{1,0,4,3,2:T(4,128)}) fusion(f32[4]{0:T(128)S(1)} %compare_convert_fusion, bf16[4,128,8,8,8]{1,0,4,3,2:T(4,128)(2,1)S(1)} %fusion.28, bf16[256,128,3,3,3]{0,4,3,2,1:T(4,128)(2,1)S(1)} %copy-done.1), kind=kOutput, calls=%fused_computation.24 | convolution fusion | flops 2794455040 | bytes 5439504 | tf_op jit(solution)/shard_map/conv_general_dilated | solution.py:37
  28.9 1.9 copy.64
  30.8 0.0 copy-start.4
  30.8 0.3 multiply_convert_fusion.1
  31.2 4.0 collective-permute-start
  35.1 1.5 collective-permute-start.1
  36.6 0.0 copy-done.4
  36.6 0.5 fusion.26
  37.1 3.0 collective-permute-done
  40.1 0.4 fusion.24
  40.5 0.0 copy-start.5
  40.5 3.4 collective-permute-done.1
  43.9 1.1 fusion.2
  44.9 0.0 copy-start.6
  45.0 0.0 copy-done.5
  45.0 1.4 convolution_convert_fusion.1
  46.4 0.0 copy-start.7
  46.4 0.0 all-gather.5.cloned.1.call-update
  46.4 0.0 all-gather.3.cloned.1.call-start
  46.5 0.0 copy-done.6
  46.5 1.4 convolution_convert_fusion.2
  47.9 0.0 all-gather.3.cloned.1.call-update
  48.0 0.0 copy-done.7
  48.0 0.5 convolution_convert_fusion
  48.4 2.5 copy.67
  50.9 0.0 copy-start.2
  50.9 112.4 %all-gather.5.cloned.1.call-done = bf16[64,4,64,512]{3,2,1,0:T(8,128)(2,1)} async-done(((bf16[4,4,64,512]{3,2,1,0:T(8,128)(2,1)}), bf16[64,4,64,512]{3,2,1,0:T(8,128)(2,1)}) %all-gather.5.cloned.1.call-update) | async-done | bytes 16777232 | tf_op jit(solution)/shard_map/all_gather | solution.py:123
  163.3 46.8 %copy.66 = bf16[64,4,64,512]{2,0,3,1:T(8,128)(2,1)} copy(bf16[64,4,64,512]{3,2,1,0:T(8,128)(2,1)} %all-gather.5.cloned.1.call-done) | data formatting | bytes 33554432 | tf_op jit(solution)/shard_map/all_gather | solution.py:123
  210.1 0.0 copy-done.2
  210.1 24.4 %bitcast_reduce_fusion = (f32[4,4,512]{0,2,1:T(8,128)}, f32[4,512,64,4]{2,3,1,0:T(4,128)}) fusion(pred[64]{0:T(512)(128)(4,1)S(1)} %iota_compare_fusion, bf16[64,4,64,512]{2,0,3,1:T(8,128)(2,1)} %copy.66, bf16[4,4,64,512]{2,0,3,1:T(4,128)(2,1)S(1)} %copy-done.2), kind=kOutput, calls=%fused_computation.1 | convolution fusion | flops 68673536 | bytes 19955776 | tf_op jit(solution)/shard_map/qhdc,khdc->qkhc/dot_general | solution.py:126
  234.5 1.4 broadcast_maximum_fusion
  235.9 30.0 %fusion.20 = f32[4,4,512]{0,2,1:T(8,128)S(1)} fusion(f32[4,4,512]{0,2,1:T(8,128)S(1)} %broadcast_maximum_fusion, f32[4,512,64,4]{2,3,1,0:T(4,128)} %get-tuple-element.9, pred[64]{0:T(512)(128)(4,1)S(1)} %iota_compare_fusion), kind=kLoop, calls=%fused_computation.34 | loop fusion | flops 2613248 | bytes 2162752 | tf_op jit(solution)/shard_map/reduce_sum | solution.py:133
  265.9 0.3 copy.70
  266.2 10.9 %all-gather.3.cloned.1.call-done = bf16[64,4,64,512]{3,2,1,0:T(8,128)(2,1)} async-done(((bf16[4,4,64,512]{3,2,1,0:T(8,128)(2,1)}), bf16[64,4,64,512]{3,2,1,0:T(8,128)(2,1)}) %all-gather.3.cloned.1.call-update) | async-done | bytes 16777232 | tf_op jit(solution)/shard_map/all_gather | solution.py:124
  277.1 46.6 %copy.68 = bf16[64,4,64,512]{2,0,3,1:T(8,128)(2,1)} copy(bf16[64,4,64,512]{3,2,1,0:T(8,128)(2,1)} %all-gather.3.cloned.1.call-done) | data formatting | bytes 33554432 | tf_op jit(solution)/shard_map/all_gather | solution.py:124
  323.7 17.5 %fusion.11 = f32[4,512,64,4]{2,3,1,0:T(4,128)} fusion(bf16[64,4,64,512]{2,0,3,1:T(8,128)(2,1)} %copy.68, f32[4,512,64,4]{2,3,1,0:T(4,128)} %get-tuple-element.9, f32[4,4,512]{0,2,1:T(8,128)S(1)} %broadcast_maximum_fusion, pred[64]{0:T(512)(128)(4,1)S(1)} %iota_compare_fusion), kind=kOutput, calls=%fused_computation.22 | convolution fusion | flops 69730304 | bytes 21004352 | tf_op jit(solution)/shard_map/qkhc,khdc->qhdc/dot_general | solution.py:134
  341.2 3.5 copy.69
  344.7 0.3 fusion.6
  345.0 0.0 copy-done
  345.0 2.3 multiply_reduce_fusion
  347.3 64.6 %psum.7 = f32[]{:T(128)} all-reduce(f32[]{:T(128)} %get-tuple-element.10), channel_id=1, replica_groups=mesh['scene'=8,'frame'=16] {'scene','frame'}, use_global_device_ids=true, to_apply=%region_4.5 | all-reduce | flops 1 | bytes 8 | tf_op jit(solution)/shard_map/psum | solution.py:143
  (4 shorter events, 0.1 us)
Async XLA Ops:
  7.2 337.9 %copy-start = (bf16[256,256]{1,0:T(8,128)(2,1)S(1)}, bf16[256,256]{1,0:T(8,128)(2,1)}, u32[]{:S(2)}) copy-start(bf16[256,256]{1,0:T(8,128)(2,1)} %param.17) | copy-start | bytes 393220
  7.2 156.1 %all-gather.5.cloned.1.call-start = ((), (), s32[]{:S(2)}) async-start(), calls=%async_computation.1 | async-start | bytes 17825792 | tf_op jit(solution)/shard_map/all_gather | solution.py:123
  10.5 2.9 copy-start.3
  16.0 5.0 %copy-start.1 = (bf16[256,128,3,3,3]{0,4,3,2,1:T(4,128)(2,1)S(1)}, bf16[256,128,3,3,3]{0,4,3,2,1:T(4,128)(2,1)}, u32[]{:S(2)}) copy-start(bf16[256,128,3,3,3]{0,4,3,2,1:T(4,128)(2,1)} %reshape.49) | copy-start | bytes 5308420
  30.8 5.8 %copy-start.4 = (bf16[3,256,256]{2,1,0:T(8,128)(2,1)S(1)}, bf16[3,256,256]{2,1,0:T(8,128)(2,1)}, u32[]{:S(2)}) copy-start(bf16[3,256,256]{2,1,0:T(8,128)(2,1)} %param.13) | copy-start | bytes 1179652
  31.2 8.9 %collective-permute-start = (bf16[1,256,512]{2,1,0:T(8,128)(2,1)S(1)}, bf16[1,256,512]{2,1,0:T(8,128)(2,1)S(1)}, u32[]{:S(2)}, u32[]{:S(2)}) collective-permute-start(bf16[1,256,512]{2,1,0:T(8,128)(2,1)S(1)} %get-tuple-element.3), channel_id=1, source_target_pairs={{0,1},{1,2},{2,3},{3,4},{4,5},{5,6},{6,7},{7,8},{8,9},{9,10},{10,1... | collective-permute-start | bytes 786440 | tf_op jit(solution)/shard_map/ppermute | solution.py:25
  35.1 8.7 %collective-permute-start.1 = (bf16[1,256,512]{2,1,0:T(8,128)(2,1)S(1)}, bf16[1,256,512]{2,1,0:T(8,128)(2,1)S(1)}, u32[]{:S(2)}, u32[]{:S(2)}) collective-permute-start(bf16[1,256,512]{2,1,0:T(8,128)(2,1)S(1)} %get-tuple-element.2), channel_id=1, source_target_pairs={{1,0},{2,1},{3,2},{4,3},{5,4},{6,5},{7,6},{8,7},{9,8},{10,9},{11,1... | collective-permute-start | bytes 786440 | tf_op jit(solution)/shard_map/ppermute | solution.py:27
  40.5 4.5 %copy-start.5 = (bf16[256,256]{1,0:T(8,128)(2,1)S(1)}, bf16[256,256]{1,0:T(8,128)(2,1)}, u32[]{:S(2)}) copy-start(bf16[256,256]{1,0:T(8,128)(2,1)} %param.15) | copy-start | bytes 393220
  44.9 1.5 copy-start.6
  46.4 1.6 copy-start.7
  46.4 230.7 %all-gather.3.cloned.1.call-start = ((), (), s32[]{:S(2)}) async-start(), calls=%async_computation | async-start | bytes 17825792 | tf_op jit(solution)/shard_map/all_gather | solution.py:124
  50.9 159.2 %copy-start.2 = (bf16[4,4,64,512]{2,0,3,1:T(4,128)(2,1)S(1)}, bf16[4,4,64,512]{2,0,3,1:T(4,128)(2,1)}, u32[]{:S(2)}) copy-start(bf16[4,4,64,512]{2,0,3,1:T(4,128)(2,1)} %copy.67) | copy-start | bytes 3145732
Sparse Core Ops, SparseCore 0:
  46.6 116.7 all-gather.4
  166.0 111.0 all-gather.2
where the time goes:
time: 423 us; the launch traced here: 421 us
  waiting for transfers between devices  130 us (31%)
  local copies, waits for them, and re-layouts  110 us (26%)
  blocking collectives  64.6 us (15%)
  matrix products  62.2 us (15%)
  other arithmetic  32 us (8%)
  between operations  16.7 us (4%)
  starting transfers between devices  5.51 us (1%)
    all_gather x1, waiting for transfers between devices, shards(): panel_keys = lax.all_gather(key_rows, 'frame', axis=0, tiled=True)  112 us
    psum x1, blocking collectives, shards(): grand_total = lax.psum(squares, ('scene', 'frame'))  64.6 us
    all_gather x1, local copies, waits for them, and re-layouts, shards(): panel_keys = lax.all_gather(key_rows, 'frame', axis=0, tiled=True)  46.8 us
    all_gather x1, local copies, waits for them, and re-layouts, shards(): panel_values = lax.all_gather(value_rows, 'frame', axis=0, tiled=True)  46.6 us
    reduce_sum x1, other arithmetic, shards(): new_sum = jnp.sum(raw_weights, axis=1)  30 us
    dot_general x1, matrix products, shards(): jnp.einsum('qhdc,khdc->qkhc', queries, panel_keys, preferred_element_type...  24.4 us
    dot_general x1, matrix products, shards(): jnp.einsum('qkhc,khdc->qhdc', raw_weights.astype(jnp.bfloat16), panel_val...  17.5 us
    conv_general_dilated x2, matrix products, spatial_conv(): lax.conv_general_dilated(voxels, kernel, (stride, stride, 1), ((1, 1), (1...  12.8 us
  transfers between devices with their start and end apart: 4, of which 4 were waited for; matrix products, arithmetic and copies ran while one was open for 26% of the time, Pallas kernels for 0%

commit v1 on v0

--- a/solution.py
+++ b/solution.py
@@ -12,6 +12,25 @@
 ZD = 8
 CELLS = 512
 NORM_EPS = 1e-06
+
+
+def gather_around(x, axis, dim):
+    size, index, rows = (lax.axis_size(axis), lax.axis_index(axis), x.shape[dim])
+    ahead = [(i, (i + 1) % size) for i in range(size)]
+    behind = [(i, (i - 1) % size) for i in range(size)]
+    out = jnp.zeros((*x.shape[:dim], size * rows, *x.shape[dim + 1 :]), x.dtype)
+    out = lax.dynamic_update_slice_in_dim(out, x, index * rows, axis=dim)
+    from_left = from_right = x
+    middle = size // 2
+    for hop in range(1, middle + 1):
+        from_left = lax.ppermute(from_left, axis, ahead)
+        out = lax.dynamic_update_slice_in_dim(out, from_left, (index - hop) % size * rows, axis=dim)
+        if hop < size - middle:
+            from_right = lax.ppermute(from_right, axis, behind)
+            out = lax.dynamic_update_slice_in_dim(
+                out, from_right, (index + hop) % size * rows, axis=dim
+            )
+    return out
 
 
 def extended(cells, sides, width):
@@ -120,7 +139,7 @@
     residual_f = temporal_block(padded, second_maps, temporal_weight)
     queries, key_rows, value_rows = project_rows(residual_f, query_weight, key_weight, value_weight)
     running_max = jnp.full((f_dev, HEADS, CELLS), -1e30, jnp.float32)
-    panel_keys = lax.all_gather(key_rows, "frame", axis=0, tiled=True)
+    panel_keys = gather_around(key_rows, "frame", 0)
     panel_values = lax.all_gather(value_rows, "frame", axis=0, tiled=True)
     count_keys = panel_keys.shape[0]
     scores = jnp.einsum(

time: 423 us -> 588 us (1.39); the launches traced: 421 us -> 578 us
  local copies, waits for them, and re-layouts: 110 us -> 173 us
  waiting for transfers between devices: 130 us -> 174 us
  starting transfers between devices: 5.51 us -> 42.5 us
  blocking collectives: 64.6 us -> 78.7 us
    ppermute x0 -> x15, waiting for transfers between devices: none -> 167 us  [the longest x8 154 us: gather_around(): from_left = lax.ppermute(from_left, axis, ahead)]
    all_gather x1 -> x0, waiting for transfers between devices: 112 us -> none  [shards(): panel_keys = lax.all_gather(key_rows, 'frame', axis=0, tiled=True)]
    ppermute x0 -> x15, local copies, waits for them, and re-layouts: none -> 50.9 us  [the longest x8 29.4 us: gather_around(): from_left = lax.ppermute(from_left, axis, ahead)]
    all_gather x1 -> x0, local copies, waits for them, and re-layouts: 46.8 us -> none  [shards(): panel_keys = lax.all_gather(key_rows, 'frame', axis=0, tiled=True)]
    dynamic_update_slice x0 -> x16, local copies, waits for them, and re-layouts: none -> 42.7 us  [the longest x8 25.4 us: gather_around(): lax.dynamic_update_slice_in_dim(out, from_left, (index - hop) % size * ro...]
    ppermute x0 -> x15, starting transfers between devices: none -> 37.1 us  [the longest x7 35.4 us: gather_around(): from_right = lax.ppermute(from_right, axis, behind)]
    psum x1, blocking collectives: 64.6 us -> 78.7 us  [shards(): grand_total = lax.psum(squares, ('scene', 'frame'))]
    broadcast_in_dim x0 -> x1, local copies, waits for them, and re-layouts: none -> 11.3 us  [gather_around(): out = jnp.zeros((*x.shape[:dim], size * rows, *x.shape[dim + 1:]), x.dtype)]
  transfers between devices with their start and end apart: 4 -> 18, of which waited for: 4 -> 11; matrix products, arithmetic and copies ran while one was open for 26% -> 29% of each run, Pallas kernels for 0% -> 0%
where the time goes in v1:
time: 588 us; the launch traced here: 578 us
  waiting for transfers between devices  174 us (30%)
  local copies, waits for them, and re-layouts  173 us (29%)
  blocking collectives  78.7 us (13%)
  matrix products  61.5 us (10%)
  starting transfers between devices  42.5 us (7%)
  other arithmetic  30.7 us (5%)
  between operations  17.4 us (3%)
    ppermute x8, waiting for transfers between devices, gather_around(): from_left = lax.ppermute(from_left, axis, ahead)  154 us
    psum x1, blocking collectives, shards(): grand_total = lax.psum(squares, ('scene', 'frame'))  78.7 us
    all_gather x1, local copies, waits for them, and re-layouts, shards(): panel_values = lax.all_gather(value_rows, 'frame', axis=0, tiled=True)  46.7 us
    ppermute x7, starting transfers between devices, gather_around(): from_right = lax.ppermute(from_right, axis, behind)  35.4 us
    reduce_sum x1, other arithmetic, shards(): new_sum = jnp.sum(raw_weights, axis=1)  30 us
    ppermute x8, local copies, waits for them, and re-layouts, gather_around(): from_left = lax.ppermute(from_left, axis, ahead)  29.4 us
    dynamic_update_slice x8, local copies, waits for them, and re-layouts, gather_around(): lax.dynamic_update_slice_in_dim(out, from_left, (index - hop) % size * ro...  25.4 us
    dot_general x1, matrix products, shards(): jnp.einsum('qhdc,khdc->qkhc', queries, panel_keys, preferred_element_type...  23.6 us
  transfers between devices with their start and end apart: 18, of which 11 were waited for; matrix products, arithmetic and copies ran while one was open for 29% of the time, Pallas kernels for 0%

profile of v1, /device:TPU:1, one launch (start us, length us, event | category | flops | bytes accessed | tf_op | source)
XLA Modules:
  0.0 578.1 jit_solution(18128440267215221369)
XLA Ops:
  7.9 2.6 copy.96
  10.6 2.9 reshape.49
  16.0 5.0 fusion.28
  21.0 7.8 %multiply_convert_fusion = (bf16[4,256,8,8,8]{1,0,4,3,2:T(4,128)(2,1)S(1)}, f32[4,256,8,8,8]{1,0,4,3,2:T(4,128)}) fusion(f32[4]{0:T(128)S(1)} %compare_convert_fusion, bf16[4,128,8,8,8]{1,0,4,3,2:T(4,128)(2,1)S(1)} %fusion.28, bf16[256,128,3,3,3]{0,4,3,2,1:T(4,128)(2,1)S(1)} %copy-done.3), kind=kOutput, calls=%fused_computation.24 | convolution fusion | flops 2794455040 | bytes 5439504 | tf_op jit(solution)/shard_map/conv_general_dilated | solution.py:56
  31.1 4.0 collective-permute-start
  37.0 3.0 collective-permute-done
  40.4 3.4 collective-permute-done.1
  48.1 3.7 collective-permute-start.3
  51.8 25.4 %collective-permute-done.2 = bf16[4,4,64,512]{3,2,1,0:T(8,128)(2,1)S(1)} collective-permute-done((bf16[4,4,64,512]{3,2,1,0:T(8,128)(2,1)S(1)}, bf16[4,4,64,512]{3,2,1,0:T(8,128)(2,1)S(1)}, u32[]{:S(2)}, u32[]{:S(2)}) %collective-permute-start.2) | collective-permute-done | bytes 1048608 | tf_op jit(solution)/shard_map/ppermute | solution.py:26
  77.2 4.1 collective-permute-done.3
  81.3 5.5 collective-permute-start.5
  86.8 25.2 %collective-permute-done.4 = bf16[4,4,64,512]{3,2,1,0:T(8,128)(2,1)S(1)} collective-permute-done((bf16[4,4,64,512]{3,2,1,0:T(8,128)(2,1)S(1)}, bf16[4,4,64,512]{3,2,1,0:T(8,128)(2,1)S(1)}, u32[]{:S(2)}, u32[]{:S(2)}) %collective-permute-start.4) | collective-permute-done | bytes 1048608 | tf_op jit(solution)/shard_map/ppermute | solution.py:26
  112.0 4.8 collective-permute-start.7
  116.8 24.2 %collective-permute-done.6 = bf16[4,4,64,512]{3,2,1,0:T(8,128)(2,1)S(1)} collective-permute-done((bf16[4,4,64,512]{3,2,1,0:T(8,128)(2,1)S(1)}, bf16[4,4,64,512]{3,2,1,0:T(8,128)(2,1)S(1)}, u32[]{:S(2)}, u32[]{:S(2)}) %collective-permute-start.6) | collective-permute-done | bytes 1048608 | tf_op jit(solution)/shard_map/ppermute | solution.py:26
  141.0 3.7 collective-permute-done.7
  144.7 5.5 collective-permute-start.9
  150.2 39.4 %collective-permute-done.8 = bf16[4,4,64,512]{3,2,1,0:T(8,128)(2,1)S(1)} collective-permute-done((bf16[4,4,64,512]{3,2,1,0:T(8,128)(2,1)S(1)}, bf16[4,4,64,512]{3,2,1,0:T(8,128)(2,1)S(1)}, u32[]{:S(2)}, u32[]{:S(2)}) %collective-permute-start.8) | collective-permute-done | bytes 1048608 | tf_op jit(solution)/shard_map/ppermute | solution.py:26
  190.6 2.7 collective-permute-done.9
  193.4 5.5 collective-permute-start.11
  198.9 40.2 %collective-permute-done.10 = bf16[4,4,64,512]{3,2,1,0:T(8,128)(2,1)} collective-permute-done((bf16[4,4,64,512]{3,2,1,0:T(8,128)(2,1)S(1)}, bf16[4,4,64,512]{3,2,1,0:T(8,128)(2,1)}, u32[]{:S(2)}, u32[]{:S(2)}) %collective-permute-start.10) | collective-permute-done | bytes 1048608 | tf_op jit(solution)/shard_map/ppermute | solution.py:26
  239.4 2.6 collective-permute-done.11
  242.0 5.6 collective-permute-start.13
  249.1 2.9 copy.100
  252.0 4.1 copy.116
  256.1 11.3 %broadcast_in_dim.37 = bf16[64,4,64,512]{2,0,3,1:T(8,128)(2,1)} broadcast(bf16[]{:T(256)} %constant.112.clone.1), dimensions={} | broadcast | bytes 16777218 | tf_op jit(solution)/shard_map/broadcast_in_dim | solution.py:21
  267.4 2.1 constant_dynamic-update-slice_fusion.15
  269.5 2.9 copy.101
  272.7 2.1 constant_dynamic-update-slice_fusion.14
  274.8 2.9 copy.102
  277.7 2.2 constant_dynamic-update-slice_fusion.13
  279.9 4.1 copy.103
  283.9 2.9 copy.104
  286.8 3.8 constant_dynamic-update-slice_fusion.12
  290.6 2.2 constant_dynamic-update-slice_fusion.11
  292.8 4.1 copy.105
  296.9 2.9 copy.106
  299.8 3.8 constant_dynamic-update-slice_fusion.10
  303.6 4.7 collective-permute-start.15
  308.3 2.1 constant_dynamic-update-slice_fusion.9
  310.5 4.1 copy.107
  314.5 2.9 copy.108
  317.4 3.7 constant_dynamic-update-slice_fusion.8
  321.2 2.2 constant_dynamic-update-slice_fusion.7
  323.4 4.5 copy.109
  327.8 2.9 copy.110
  330.7 3.8 constant_dynamic-update-slice_fusion.6
  334.5 2.2 constant_dynamic-update-slice_fusion.5
  336.7 4.1 copy.111
  340.8 2.9 copy.112
  343.7 3.7 constant_dynamic-update-slice_fusion.4
  347.4 2.1 constant_dynamic-update-slice_fusion.3
  349.5 2.9 copy.113
  352.5 4.1 copy.114
  356.5 2.2 constant_dynamic-update-slice_fusion.2
  358.7 2.2 constant_dynamic-update-slice_fusion.1
  361.0 2.9 copy.115
  363.9 2.2 constant_dynamic-update-slice_fusion
  366.1 23.6 %bitcast_reduce_fusion = (f32[4,4,512]{0,2,1:T(8,128)S(1)}, f32[4,512,64,4]{2,3,1,0:T(4,128)}) fusion(pred[64]{0:T(512)(128)(4,1)S(1)} %iota_compare_fusion, bf16[64,4,64,512]{2,0,3,1:T(8,128)(2,1)} %constant_dynamic-update-slice_fusion, bf16[4,4,64,512]{2,0,3,1:T(4,128)(2,1)} %copy.116), kind=kOutput, calls=%fused_computation.1 | convolution fusion | flops 68673536 | bytes 19955776 | tf_op jit(solution)/shard_map/qhdc,khdc->qkhc/dot_general | solution.py:145
  389.8 30.0 %fusion.20 = f32[4,4,512]{0,2,1:T(8,128)S(1)} fusion(f32[4,4,512]{0,2,1:T(8,128)S(1)} %broadcast_maximum_fusion, f32[4,512,64,4]{2,3,1,0:T(4,128)} %get-tuple-element.9, pred[64]{0:T(512)(128)(4,1)S(1)} %iota_compare_fusion), kind=kLoop, calls=%fused_computation.34 | loop fusion | flops 2613248 | bytes 2162752 | tf_op jit(solution)/shard_map/reduce_sum | solution.py:152
  420.2 46.7 %copy.117 = bf16[64,4,64,512]{2,0,3,1:T(8,128)(2,1)} copy(bf16[64,4,64,512]{3,2,1,0:T(8,128)(2,1)} %all-gather.2.cloned.1.call-done) | data formatting | bytes 33554432 | tf_op jit(solution)/shard_map/all_gather | solution.py:143
  466.9 17.6 %fusion.11 = f32[4,512,64,4]{2,3,1,0:T(4,128)} fusion(bf16[64,4,64,512]{2,0,3,1:T(8,128)(2,1)} %copy.117, f32[4,512,64,4]{2,3,1,0:T(4,128)} %get-tuple-element.9, f32[4,4,512]{0,2,1:T(8,128)S(1)} %broadcast_maximum_fusion, pred[64]{0:T(512)(128)(4,1)S(1)} %iota_compare_fusion), kind=kOutput, calls=%fused_computation.22 | convolution fusion | flops 69730304 | bytes 21004352 | tf_op jit(solution)/shard_map/qkhc,khdc->qhdc/dot_general | solution.py:153
  484.5 3.5 copy.118
  488.3 2.3 multiply_reduce_fusion
  490.6 78.7 %psum.7 = f32[]{:T(128)} all-reduce(f32[]{:T(128)} %get-tuple-element.10), channel_id=1, replica_groups=mesh['scene'=8,'frame'=16] {'scene','frame'}, use_global_device_ids=true, to_apply=%region_4.5 | all-reduce | flops 1 | bytes 8 | tf_op jit(solution)/shard_map/psum | solution.py:162
  (69 shorter events, 15.2 us)
Async XLA Ops:
  7.2 481.1 %copy-start = (bf16[256,256]{1,0:T(8,128)(2,1)S(1)}, bf16[256,256]{1,0:T(8,128)(2,1)}, u32[]{:S(2)}) copy-start(bf16[256,256]{1,0:T(8,128)(2,1)} %param.17) | copy-start | bytes 393220
  7.2 413.0 %all-gather.2.cloned.1.call-start = ((), (), s32[]{:S(2)}) async-start(), calls=%async_computation | async-start | bytes 17825792 | tf_op jit(solution)/shard_map/all_gather | solution.py:143
  10.5 2.9 copy-start.4
  16.0 5.0 copy-start.3
  30.7 5.8 %copy-start.13 = (bf16[3,256,256]{2,1,0:T(8,128)(2,1)S(1)}, bf16[3,256,256]{2,1,0:T(8,128)(2,1)}, u32[]{:S(2)}) copy-start(bf16[3,256,256]{2,1,0:T(8,128)(2,1)} %param.13) | copy-start | bytes 1179652
  31.1 8.9 %collective-permute-start = (bf16[1,256,512]{2,1,0:T(8,128)(2,1)S(1)}, bf16[1,256,512]{2,1,0:T(8,128)(2,1)S(1)}, u32[]{:S(2)}, u32[]{:S(2)}) collective-permute-start(bf16[1,256,512]{2,1,0:T(8,128)(2,1)S(1)} %get-tuple-element.3), channel_id=1, source_target_pairs={{0,1},{1,2},{2,3},{3,4},{4,5},{5,6},{6,7},{7,8},{8,9},{9,10},{10,1... | collective-permute-start | bytes 786440 | tf_op jit(solution)/shard_map/ppermute | solution.py:44
  35.0 8.8 %collective-permute-start.1 = (bf16[1,256,512]{2,1,0:T(8,128)(2,1)S(1)}, bf16[1,256,512]{2,1,0:T(8,128)(2,1)S(1)}, u32[]{:S(2)}, u32[]{:S(2)}) collective-permute-start(bf16[1,256,512]{2,1,0:T(8,128)(2,1)S(1)} %get-tuple-element.2), channel_id=1, source_target_pairs={{1,0},{2,1},{3,2},{4,3},{5,4},{6,5},{7,6},{8,7},{9,8},{10,9},{11,1... | collective-permute-start | bytes 786440 | tf_op jit(solution)/shard_map/ppermute | solution.py:46
  40.4 4.5 copy-start.14
  44.8 1.5 copy-start.15
  46.3 201.3 %copy-start.16 = (bf16[256,256]{1,0:T(8,128)(2,1)S(1)}, bf16[256,256]{1,0:T(8,128)(2,1)}, u32[]{:S(2)}) copy-start(bf16[256,256]{1,0:T(8,128)(2,1)} %param.14) | copy-start | bytes 393220
  46.8 1.3 copy-start.2
  46.8 30.4 %collective-permute-start.2 = (bf16[4,4,64,512]{3,2,1,0:T(8,128)(2,1)S(1)}, bf16[4,4,64,512]{3,2,1,0:T(8,128)(2,1)S(1)}, u32[]{:S(2)}, u32[]{:S(2)}) collective-permute-start(bf16[4,4,64,512]{3,2,1,0:T(8,128)(2,1)S(1)} %bitcast.87), channel_id=1, source_target_pairs={{0,1},{1,2},{2,3},{3,4},{4,5},{5,6},{6,7},{7,8},{8,9},{9,10},{10,1... | collective-permute-start | bytes 3145736 | tf_op jit(solution)/shard_map/ppermute | solution.py:26
  48.1 33.2 %collective-permute-start.3 = (bf16[4,4,64,512]{3,2,1,0:T(8,128)(2,1)S(1)}, bf16[4,4,64,512]{3,2,1,0:T(8,128)(2,1)S(1)}, u32[]{:S(2)}, u32[]{:S(2)}) collective-permute-start(bf16[4,4,64,512]{3,2,1,0:T(8,128)(2,1)S(1)} %bitcast.88), channel_id=1, source_target_pairs={{0,15},{1,0},{2,1},{3,2},{4,3},{5,4},{6,5},{7,6},{8,7},{9,8},{10,9... | collective-permute-start | bytes 3145736 | tf_op jit(solution)/shard_map/ppermute | solution.py:29
  77.2 9.6 %copy-start.12 = (bf16[4,4,64,512]{3,2,1,0:T(8,128)(2,1)}, bf16[4,4,64,512]{3,2,1,0:T(8,128)(2,1)S(1)}, u32[]{:S(2)}) copy-start(bf16[4,4,64,512]{3,2,1,0:T(8,128)(2,1)S(1)} %collective-permute-done.2) | copy-start | bytes 3145732
  77.2 34.8 %collective-permute-start.4 = (bf16[4,4,64,512]{3,2,1,0:T(8,128)(2,1)S(1)}, bf16[4,4,64,512]{3,2,1,0:T(8,128)(2,1)S(1)}, u32[]{:S(2)}, u32[]{:S(2)}) collective-permute-start(bf16[4,4,64,512]{3,2,1,0:T(8,128)(2,1)S(1)} %collective-permute-done.2), channel_id=1, source_target_pairs={{0,1},{1,2},{2,3},{3,4},{4,5},{5,6},{6,7},{7,8},{8,9},{9,10},{10,1... | collective-permute-start | bytes 3145736 | tf_op jit(solution)/shard_map/ppermute | solution.py:26
  81.3 35.5 %copy-start.6 = (bf16[4,4,64,512]{3,2,1,0:T(8,128)(2,1)}, bf16[4,4,64,512]{3,2,1,0:T(8,128)(2,1)S(1)}, u32[]{:S(2)}) copy-start(bf16[4,4,64,512]{3,2,1,0:T(8,128)(2,1)S(1)} %collective-permute-done.3) | copy-start | bytes 3145732
  81.3 30.7 %collective-permute-start.5 = (bf16[4,4,64,512]{3,2,1,0:T(8,128)(2,1)S(1)}, bf16[4,4,64,512]{3,2,1,0:T(8,128)(2,1)S(1)}, u32[]{:S(2)}, u32[]{:S(2)}) collective-permute-start(bf16[4,4,64,512]{3,2,1,0:T(8,128)(2,1)S(1)} %collective-permute-done.3), channel_id=1, source_target_pairs={{0,15},{1,0},{2,1},{3,2},{4,3},{5,4},{6,5},{7,6},{8,7},{9,8},{10,9... | collective-permute-start | bytes 3145736 | tf_op jit(solution)/shard_map/ppermute | solution.py:29
  112.0 127.0 %copy-start.7 = (bf16[4,4,64,512]{3,2,1,0:T(8,128)(2,1)}, bf16[4,4,64,512]{3,2,1,0:T(8,128)(2,1)S(1)}, u32[]{:S(2)}) copy-start(bf16[4,4,64,512]{3,2,1,0:T(8,128)(2,1)S(1)} %collective-permute-done.4) | copy-start | bytes 3145732
  112.0 28.9 %collective-permute-start.6 = (bf16[4,4,64,512]{3,2,1,0:T(8,128)(2,1)S(1)}, bf16[4,4,64,512]{3,2,1,0:T(8,128)(2,1)S(1)}, u32[]{:S(2)}, u32[]{:S(2)}) collective-permute-start(bf16[4,4,64,512]{3,2,1,0:T(8,128)(2,1)S(1)} %collective-permute-done.4), channel_id=1, source_target_pairs={{0,1},{1,2},{2,3},{3,4},{4,5},{5,6},{6,7},{7,8},{8,9},{9,10},{10,1... | collective-permute-start | bytes 3145736 | tf_op jit(solution)/shard_map/ppermute | solution.py:26
  112.0 127.0 %copy-start.10 = (bf16[4,4,64,512]{3,2,1,0:T(8,128)(2,1)}, bf16[4,4,64,512]{3,2,1,0:T(8,128)(2,1)S(1)}, u32[]{:S(2)}) copy-start(bf16[4,4,64,512]{3,2,1,0:T(8,128)(2,1)S(1)} %collective-permute-done.5) | copy-start | bytes 3145732
  112.0 32.7 %collective-permute-start.7 = (bf16[4,4,64,512]{3,2,1,0:T(8,128)(2,1)S(1)}, bf16[4,4,64,512]{3,2,1,0:T(8,128)(2,1)S(1)}, u32[]{:S(2)}, u32[]{:S(2)}) collective-permute-start(bf16[4,4,64,512]{3,2,1,0:T(8,128)(2,1)S(1)} %collective-permute-done.5), channel_id=1, source_target_pairs={{0,15},{1,0},{2,1},{3,2},{4,3},{5,4},{6,5},{7,6},{8,7},{9,8},{10,9... | collective-permute-start | bytes 3145736 | tf_op jit(solution)/shard_map/ppermute | solution.py:29
  141.0 98.1 %copy-start.8 = (bf16[4,4,64,512]{3,2,1,0:T(8,128)(2,1)}, bf16[4,4,64,512]{3,2,1,0:T(8,128)(2,1)S(1)}, u32[]{:S(2)}) copy-start(bf16[4,4,64,512]{3,2,1,0:T(8,128)(2,1)S(1)} %collective-permute-done.6) | copy-start | bytes 3145732
  141.0 48.6 %collective-permute-start.8 = (bf16[4,4,64,512]{3,2,1,0:T(8,128)(2,1)S(1)}, bf16[4,4,64,512]{3,2,1,0:T(8,128)(2,1)S(1)}, u32[]{:S(2)}, u32[]{:S(2)}) collective-permute-start(bf16[4,4,64,512]{3,2,1,0:T(8,128)(2,1)S(1)} %collective-permute-done.6), channel_id=1, source_target_pairs={{0,1},{1,2},{2,3},{3,4},{4,5},{5,6},{6,7},{7,8},{8,9},{9,10},{10,1... | collective-permute-start | bytes 3145736 | tf_op jit(solution)/shard_map/ppermute | solution.py:26
  144.7 94.3 %copy-start.11 = (bf16[4,4,64,512]{3,2,1,0:T(8,128)(2,1)}, bf16[4,4,64,512]{3,2,1,0:T(8,128)(2,1)S(1)}, u32[]{:S(2)}) copy-start(bf16[4,4,64,512]{3,2,1,0:T(8,128)(2,1)S(1)} %collective-permute-done.7) | copy-start | bytes 3145732
  144.7 48.6 %collective-permute-start.9 = (bf16[4,4,64,512]{3,2,1,0:T(8,128)(2,1)S(1)}, bf16[4,4,64,512]{3,2,1,0:T(8,128)(2,1)S(1)}, u32[]{:S(2)}, u32[]{:S(2)}) collective-permute-start(bf16[4,4,64,512]{3,2,1,0:T(8,128)(2,1)S(1)} %collective-permute-done.7), channel_id=1, source_target_pairs={{0,15},{1,0},{2,1},{3,2},{4,3},{5,4},{6,5},{7,6},{8,7},{9,8},{10,9... | collective-permute-start | bytes 3145736 | tf_op jit(solution)/shard_map/ppermute | solution.py:29
  189.6 1.0 copy-start.5
  190.6 48.4 %collective-permute-start.10 = (bf16[4,4,64,512]{3,2,1,0:T(8,128)(2,1)S(1)}, bf16[4,4,64,512]{3,2,1,0:T(8,128)(2,1)}, u32[]{:S(2)}, u32[]{:S(2)}) collective-permute-start(bf16[4,4,64,512]{3,2,1,0:T(8,128)(2,1)S(1)} %collective-permute-done.8), channel_id=1, source_target_pairs={{0,1},{1,2},{2,3},{3,4},{4,5},{5,6},{6,7},{7,8},{8,9},{9,10},{10,1... | collective-permute-start | bytes 3145736 | tf_op jit(solution)/shard_map/ppermute | solution.py:26
  193.4 54.3 %copy-start.9 = (bf16[4,4,64,512]{3,2,1,0:T(8,128)(2,1)}, bf16[4,4,64,512]{3,2,1,0:T(8,128)(2,1)S(1)}, u32[]{:S(2)}) copy-start(bf16[4,4,64,512]{3,2,1,0:T(8,128)(2,1)S(1)} %collective-permute-done.9) | copy-start | bytes 3145732
  193.4 48.6 %collective-permute-start.11 = (bf16[4,4,64,512]{3,2,1,0:T(8,128)(2,1)S(1)}, bf16[4,4,64,512]{3,2,1,0:T(8,128)(2,1)}, u32[]{:S(2)}, u32[]{:S(2)}) collective-permute-start(bf16[4,4,64,512]{3,2,1,0:T(8,128)(2,1)S(1)} %collective-permute-done.9), channel_id=1, source_target_pairs={{0,15},{1,0},{2,1},{3,2},{4,3},{5,4},{6,5},{7,6},{8,7},{9,8},{10,9... | collective-permute-start | bytes 3145736 | tf_op jit(solution)/shard_map/ppermute | solution.py:29
  239.1 33.3 %collective-permute-start.12 = (bf16[4,4,64,512]{3,2,1,0:T(8,128)(2,1)}, bf16[4,4,64,512]{3,2,1,0:T(8,128)(2,1)}, u32[]{:S(2)}, u32[]{:S(2)}) collective-permute-start(bf16[4,4,64,512]{3,2,1,0:T(8,128)(2,1)} %collective-permute-done.10), channel_id=1, source_target_pairs={{0,1},{1,2},{2,3},{3,4},{4,5},{5,6},{6,7},{7,8},{8,9},{9,10},{10,1... | collective-permute-start | bytes 3145736 | tf_op jit(solution)/shard_map/ppermute | solution.py:26
  242.0 61.6 %collective-permute-start.13 = (bf16[4,4,64,512]{3,2,1,0:T(8,128)(2,1)}, bf16[4,4,64,512]{3,2,1,0:T(8,128)(2,1)}, u32[]{:S(2)}, u32[]{:S(2)}) collective-permute-start(bf16[4,4,64,512]{3,2,1,0:T(8,128)(2,1)} %collective-permute-done.11), channel_id=1, source_target_pairs={{0,15},{1,0},{2,1},{3,2},{4,3},{5,4},{6,5},{7,6},{8,7},{9,8},{10,9... | collective-permute-start | bytes 3145736 | tf_op jit(solution)/shard_map/ppermute | solution.py:29
  272.4 48.8 %collective-permute-start.14 = (bf16[4,4,64,512]{3,2,1,0:T(8,128)(2,1)}, bf16[4,4,64,512]{3,2,1,0:T(8,128)(2,1)}, u32[]{:S(2)}, u32[]{:S(2)}) collective-permute-start(bf16[4,4,64,512]{3,2,1,0:T(8,128)(2,1)} %collective-permute-done.12), channel_id=1, source_target_pairs={{0,1},{1,2},{2,3},{3,4},{4,5},{5,6},{6,7},{7,8},{8,9},{9,10},{10,1... | collective-permute-start | bytes 3145736 | tf_op jit(solution)/shard_map/ppermute | solution.py:26
  303.6 48.8 %collective-permute-start.15 = (bf16[4,4,64,512]{3,2,1,0:T(8,128)(2,1)}, bf16[4,4,64,512]{3,2,1,0:T(8,128)(2,1)}, u32[]{:S(2)}, u32[]{:S(2)}) collective-permute-start(bf16[4,4,64,512]{3,2,1,0:T(8,128)(2,1)} %collective-permute-done.13), channel_id=1, source_target_pairs={{0,15},{1,0},{2,1},{3,2},{4,3},{5,4},{6,5},{7,6},{8,7},{9,8},{10,9... | collective-permute-start | bytes 3145736 | tf_op jit(solution)/shard_map/ppermute | solution.py:29
  321.2 39.8 %collective-permute-start.16 = (bf16[4,4,64,512]{3,2,1,0:T(8,128)(2,1)}, bf16[4,4,64,512]{3,2,1,0:T(8,128)(2,1)}, u32[]{:S(2)}, u32[]{:S(2)}) collective-permute-start(bf16[4,4,64,512]{3,2,1,0:T(8,128)(2,1)} %collective-permute-done.14), channel_id=1, source_target_pairs={{0,1},{1,2},{2,3},{3,4},{4,5},{5,6},{6,7},{7,8},{8,9},{9,10},{10,1... | collective-permute-start | bytes 3145736 | tf_op jit(solution)/shard_map/ppermute | solution.py:26
  356.5 2.2 copy-start.1
Sparse Core Ops, SparseCore 0:
  46.5 209.5 all-gather.1
